TPU v7x, 128 devices: a whole 4x4x4 slice. The times are simulated.
128 devices in a mesh: wide: 32 (over x, y, z_lo), narrow: 4 (over z_hi, core).
Axes of the slice: x: 4, y: 4, z: 4 (z_hi: 2, z_lo: 2; z = z_hi * 2 + z_lo), core: 2. Of those that a mesh axis runs over, the one named last changes fastest.
Arguments:
- queries: bfloat16 [98304, 768], P(('wide', 'narrow')), may hold values from -24 to 24
- labels: bfloat16 [98304, 768], P(('wide', 'narrow')), may hold values from -24 to 24
- logit_scale: float32 [1], replicated, may hold values from 2 to 3
Outputs:
- loss: float32 [98304], P(('wide', 'narrow'))
- query_grad: bfloat16 [98304, 768], P(('wide', 'narrow'))
- label_grad: bfloat16 [98304, 768], P(('wide', 'narrow'))
All inputs are finite; a program needn't handle non-finite values.
Results may differ from a plain program's by a relative error of at most 0.004.
Values may be sent and summed in bfloat16 or wider, within the bound.
A program may use at most 128 MiB of HBM per device.

v0:
```python
import math

import jax
import jax.numpy as jnp
from jax import lax
from jax.sharding import PartitionSpec as P


def from_behind(block, axis, distance):
    devices = range(lax.axis_size(axis))
    route = [((i - distance) % len(devices), i) for i in devices]
    return lax.ppermute(block, axis, route)


def local(queries, labels, logit_scale):
    rows = queries.shape[0]
    width = queries.shape[1]
    groups = lax.axis_size("narrow")
    block = rows * groups
    own_labels = lax.all_gather(labels, "narrow", axis=0, tiled=True)
    prev_labels = from_behind(own_labels, "wide", 1)
    window = jnp.concatenate([own_labels, prev_labels], axis=0)
    factor = logit_scale[0] / math.sqrt(width)
    scores = jnp.dot(queries, window.T, preferred_element_type=jnp.float32) * factor
    top = jnp.max(scores, axis=1, keepdims=True)
    lse = top[:, 0] + jnp.log(jnp.sum(jnp.exp(scores - top), axis=1))
    columns = jnp.arange(2 * block, dtype=jnp.int32)
    positive = lax.axis_index("narrow") * rows + jnp.arange(rows, dtype=jnp.int32)
    hit = columns[None, :] == positive[:, None]
    loss = lse - jnp.sum(jnp.where(hit, scores, 0.0), axis=1)
    weights = (jnp.exp(scores - lse[:, None]) - hit.astype(jnp.float32)).astype(jnp.bfloat16)
    query_grad = jnp.dot(weights, window, preferred_element_type=jnp.float32).astype(jnp.bfloat16)
    prev_whole = jnp.einsum(
        "rc,rd->cd", weights[:, block:], queries, preferred_element_type=jnp.float32
    )
    returned = from_behind(prev_whole.astype(jnp.bfloat16), "wide", -1).astype(prev_whole.dtype)
    picked = lax.dynamic_slice_in_dim(weights, jnp.int32(0), lax.axis_size("narrow") * rows, 1)
    label_grad = lax.psum_scatter(
        jnp.einsum("rc,rd->cd", picked, queries, preferred_element_type=jnp.float32) + returned,
        "narrow",
        scatter_dimension=0,
        tiled=True,
    )
    return (loss, query_grad, label_grad.astype(jnp.bfloat16))


def solution(mesh):
    in_specs = (P(("wide", "narrow"), None), P(("wide", "narrow"), None), P())
    out_specs = (P(("wide", "narrow")), P(("wide", "narrow"), None), P(("wide", "narrow"), None))
    return jax.shard_map(local, mesh=mesh, in_specs=in_specs, out_specs=out_specs, check_vma=False)
```

profile of v0, /device:TPU:1, one launch (start us, length us, event | category | flops | bytes accessed | tf_op | source)
XLA Modules:
  0.0 403.3 jit_solution(12586211823689910148)
XLA Ops:
  7.2 0.0 copy-start
  7.2 0.0 all-gather.2.cloned.1.call-start
  7.2 0.7 all-gather.2.cloned.1.call-update
  7.9 0.0 reduce-scatter.2.cloned.1.call-start
  8.0 47.0 %all-gather.2.cloned.1.call-done = bf16[3072,768]{1,0:T(8,128)(2,1)} async-done(((bf16[768,768]{1,0:T(8,128)(2,1)}), bf16[3072,768]{1,0:T(8,128)(2,1)}) %all-gather.2.cloned.1.call-update) | async-done | bytes 4718608 | tf_op jit(solution)/shard_map/all_gather | solution.py:20
  55.0 0.4 collective-permute-start
  56.0 2.6 constant_dynamic-update-slice_fusion.1
  58.7 104.0 %collective-permute-done = bf16[3072,768]{1,0:T(8,128)(2,1)} collective-permute-done((bf16[3072,768]{1,0:T(8,128)(2,1)}, bf16[3072,768]{1,0:T(8,128)(2,1)}, u32[]{:S(2)}, u32[]{:S(2)}) %collective-permute-start) | collective-permute-done | bytes 4718624 | tf_op jit(solution)/shard_map/ppermute | solution.py:12
  162.7 2.6 constant_dynamic-update-slice_fusion
  165.3 0.0 copy-start.2
  165.3 3.6 copy-done.2
  168.9 0.0 copy-done
  168.9 10.4 %multiply_reduce_fusion = (f32[768]{0:T(1024)S(1)}, f32[6144,768]{1,0:T(8,128)S(1)}) fusion(f32[]{:T(128)} %bitcast, bf16[6144,768]{1,0:T(8,128)(2,1)} %copy-done.2, bf16[768,768]{1,0:T(8,128)(2,1)S(1)} %copy-done), kind=kOutput, calls=%fused_computation.10 | convolution fusion | flops 7257193472 | bytes 29494276 | tf_op jit(solution)/shard_map/dot_general | solution.py:24
  179.3 5.5 %fusion.2 = (f32[768]{0:T(1024)S(1)}, f32[768]{0:T(1024)S(1)}) fusion(f32[6144,768]{1,0:T(8,128)S(1)} %get-tuple-element.8, s32[768]{0:T(1024)S(1)} %iota_add_fusion, f32[]{:T(128)} %bitcast, f32[768]{0:T(1024)S(1)} %get-tuple-element.7), kind=kLoop, calls=%fused_computation.5 | loop fusion | flops 28310016 | bytes 18886660 | tf_op jit(solution)/shard_map/reduce_sum | solution.py:30
  184.9 0.6 fusion.11
  185.5 7.0 %fusion.5 = bf16[768,6144]{0,1:T(8,128)(2,1)} fusion(f32[6144,768]{1,0:T(8,128)S(1)} %get-tuple-element.8, f32[768]{0:T(1024)S(1)} %get-tuple-element.6, s32[768]{0:T(1024)S(1)} %iota_add_fusion, f32[]{:T(128)} %bitcast), kind=kLoop, calls=%fused_computation.8 | loop fusion | flops 28311552 | bytes 28317700 | tf_op jit(solution)/shard_map/convert_element_type | solution.py:31
  192.4 0.0 copy-start.1
  192.4 6.7 %convolution_convert_fusion = bf16[3072,768]{1,0:T(8,128)(2,1)S(1)} fusion(bf16[768,768]{1,0:T(8,128)(2,1)S(1)} %copy-done, bf16[768,6144]{0,1:T(8,128)(2,1)} %fusion.5), kind=kOutput, calls=%fused_computation.12 | convolution fusion | flops 3626237952 | bytes 10616832 | tf_op jit(solution)/shard_map/rc,rd->cd/dot_general | solution.py:33
  199.2 0.7 collective-permute-start.1
  199.9 101.8 %collective-permute-done.1 = bf16[3072,768]{1,0:T(8,128)(2,1)S(1)} collective-permute-done((bf16[3072,768]{1,0:T(8,128)(2,1)S(1)}, bf16[3072,768]{1,0:T(8,128)(2,1)S(1)}, u32[]{:S(2)}, u32[]{:S(2)}) %collective-permute-start.1) | collective-permute-done | bytes 4718624 | tf_op jit(solution)/shard_map/ppermute | solution.py:12
  301.6 0.0 copy-done.1
  301.6 6.4 %convert_add_fusion = f32[3072,768]{1,0:T(8,128)} fusion(bf16[3072,768]{1,0:T(8,128)(2,1)S(1)} %collective-permute-done.1, bf16[768,768]{1,0:T(8,128)(2,1)S(1)} %copy-done, bf16[768,6144]{0,1:T(8,128)(2,1)S(1)} %copy-done.1), kind=kOutput, calls=%fused_computation.11 | convolution fusion | flops 3628597248 | bytes 20054016 | tf_op jit(solution)/shard_map/rc,rd->cd/dot_general | solution.py:39
  308.0 0.0 reduce-scatter.2.cloned.1.call-update
  308.1 13.7 %convolution_convert_fusion.1 = bf16[768,768]{1,0:T(8,128)(2,1)} fusion(bf16[768,6144]{0,1:T(8,128)(2,1)} %fusion.5, bf16[6144,768]{1,0:T(8,128)(2,1)} %copy-done.2), kind=kOutput, calls=%fused_computation.16 | convolution fusion | flops 7248347136 | bytes 20054016 | tf_op jit(solution)/shard_map/dot_general | solution.py:32
  321.8 71.9 %reduce-scatter.2.cloned.1.call-done = f32[768,768]{1,0:T(8,128)} async-done(((f32[3072,768]{1,0:T(8,128)}), f32[768,768]{1,0:T(8,128)}) %reduce-scatter.2.cloned.1.call-update) | async-done | bytes 2359312 | tf_op jit(solution)/shard_map/reduce_scatter | solution.py:38
  393.7 2.8 convert_element_type.23
  (1 shorter events, 0.0 us)
Async XLA Ops:
  7.2 161.8 %copy-start = (bf16[768,768]{1,0:T(8,128)(2,1)S(1)}, bf16[768,768]{1,0:T(8,128)(2,1)}, u32[]{:S(2)}) copy-start(bf16[768,768]{1,0:T(8,128)(2,1)} %param.3) | copy-start | bytes 3538948
  7.2 47.8 %all-gather.2.cloned.1.call-start = ((), (), s32[]{:S(2)}) async-start(), calls=%async_computation.1 | async-start | bytes 5898240 | tf_op jit(solution)/shard_map/all_gather | solution.py:20
  7.9 385.7 %reduce-scatter.2.cloned.1.call-start = ((), (), s32[]{:S(2)}) async-start(), calls=%async_computation.2 | async-start | bytes 11796480 | tf_op jit(solution)/shard_map/reduce_scatter | solution.py:38
  55.0 107.7 %collective-permute-start = (bf16[3072,768]{1,0:T(8,128)(2,1)}, bf16[3072,768]{1,0:T(8,128)(2,1)}, u32[]{:S(2)}, u32[]{:S(2)}) collective-permute-start(bf16[3072,768]{1,0:T(8,128)(2,1)} %all-gather.2.cloned.1.call-done), channel_id=1, source_target_pairs={{124,0},{0,4},{4,8},{8,12},{12,16},{16,20},{20,24},{24,28},{28,32}... | collective-permute-start | bytes 14155784 | tf_op jit(solution)/shard_map/ppermute | solution.py:12
  165.3 3.6 copy-start.2
  192.4 109.2 %copy-start.1 = (bf16[768,6144]{0,1:T(8,128)(2,1)S(1)}, bf16[768,6144]{0,1:T(8,128)(2,1)}, u32[]{:S(2)}) copy-start(bf16[768,6144]{0,1:T(8,128)(2,1)} %fusion.5) | copy-start | bytes 28311556
  199.2 102.5 %collective-permute-start.1 = (bf16[3072,768]{1,0:T(8,128)(2,1)S(1)}, bf16[3072,768]{1,0:T(8,128)(2,1)S(1)}, u32[]{:S(2)}, u32[]{:S(2)}) collective-permute-start(bf16[3072,768]{1,0:T(8,128)(2,1)S(1)} %convolution_convert_fusion), channel_id=1, source_target_pairs={{4,0},{8,4},{12,8},{16,12},{20,16},{24,20},{28,24},{32,28},{36,32}... | collective-permute-start | bytes 14155784 | tf_op jit(solution)/shard_map/ppermute | solution.py:12
Sparse Core Ops, SparseCore 0:
  9.7 45.2 all-gather.1
  308.2 85.4 reduce-scatter.1
where the time goes:
time: 404 us; the launch traced here: 403 us
  waiting for transfers between devices  325 us (80%)
  matrix products  37.2 us (9%)
  other arithmetic  15.9 us (4%)
  between operations  14.7 us (4%)
  local copies, waits for them, and re-layouts  8.91 us (2%)
    ppermute x2, waiting for transfers between devices, from_behind(): return lax.ppermute(block, axis, route)  206 us
    reduce_scatter x1, waiting for transfers between devices, local(): lax.psum_scatter(jnp.einsum('rc,rd->cd', picked, queries, preferred_eleme...  71.9 us
    all_gather x1, waiting for transfers between devices, local(): own_labels = lax.all_gather(labels, 'narrow', axis=0, tiled=True)  47 us
    dot_general x1, matrix products, local(): jnp.dot(weights, window, preferred_element_type=jnp.float32)  13.7 us
    dot_general x1, matrix products, local(): jnp.dot(queries, window.T, preferred_element_type=jnp.float32) * factor  10.4 us
  transfers between devices with their start and end apart: 4, of which 4 were waited for; matrix products, arithmetic and copies ran while one was open for 4% of the time, Pallas kernels for 0%

commit v1 on v0

v1 whole, which is shorter than its diff:
```python
import functools
import math

import jax
import jax.numpy as jnp
from jax import lax
from jax.experimental import pallas as pl
from jax.experimental.pallas import tpu as pltpu
from jax.sharding import PartitionSpec as P

MESH = pl.DeviceIdType.MESH
F32, BF16 = jnp.float32, jnp.bfloat16
CH = 256
SUB = 64
NT = (((1,), (1,)), ((), ()))
NN = (((1,), (0,)), ((), ()))
TN = (((0,), (0,)), ((), ()))


def kernel(
    scale_ref, q_ref, l_ref, loss_ref, qg_ref, lg_ref,
    QB, LB, E, MX, SM, AL, ST, RS, SII, ACC, QGT, QG0,
    YS, LS, QS, DS3, DS1, YR, LR, QR, DR2, DR0, QO, LO,
    s_in, s_out, s_q, r_q, s_l, r_l, s_y, r_y, s_1, r_1, s_3, r_3, s_st, r_st,
    s_yr, r_yr, s_d3, r_d3, s_qz, r_qz, s_lz, r_lz, s_d1, r_d1,
):
    rows = q_ref.shape[0]
    nk, ns = rows // CH, rows // SUB
    per = CH // SUB
    w, n = lax.axis_index("wide"), lax.axis_index("narrow")
    nw = lax.axis_size("wide")
    par = lax.rem(w, 2)
    wx = w + 1 - 2 * par
    nc = n + 1 - 2 * lax.rem(n, 2)
    dev_q, dev_l = (wx, n), (wx, lax.rem(n + 2, 4))
    dev_d, dev_qd = (w, nc), (wx, nc)
    dev_yf, dev_yb = (lax.rem(w + 2, nw), n), (lax.rem(w + nw - 2, nw), n)
    even, odd = par == 0, par == 1
    factor = scale_ref[0] * (1.0 / math.sqrt(q_ref.shape[1]))

    def sub(i):
        return pl.ds(pl.multiple_of(i * SUB, SUB), SUB)

    def chunk(c):
        return pl.ds(pl.multiple_of(c * CH, CH), CH)

    def rc(src, dst, ssem, rsem, dev):
        return pltpu.make_async_remote_copy(
            src_ref=src, dst_ref=dst, send_sem=ssem, recv_sem=rsem, device_id=dev, device_id_type=MESH
        )

    def c_q(i):
        return rc(q_ref.at[sub(i)], QB.at[2, sub(i)], s_q.at[i], r_q.at[i], dev_q)

    def c_l(i):
        return rc(l_ref.at[sub(i)], LB.at[1, sub(i)], s_l.at[i], r_l.at[i], dev_l)

    def c_y(i):
        return rc(LB.at[1 - par, sub(i)], LB.at[2, sub(i)], s_y.at[i], r_y.at[i], dev_yf)

    def c_1():
        return rc(q_ref, QB.at[1], s_1.at[0], r_1.at[0], dev_d)

    def c_3(i):
        return rc(QB.at[2, sub(i)], QB.at[3, sub(i)], s_3.at[i], r_3.at[i], dev_d)

    def c_st(j):
        return rc(ST, RS.at[j], s_st.at[j], r_st.at[j], (dev_d, dev_q, dev_qd)[j])

    def c_yr(i):
        return rc(YS.at[sub(i)], YR.at[sub(i)], s_yr.at[i], r_yr.at[i], dev_yb)

    def c_d3(c):
        return rc(DS3.at[chunk(c)], DR2.at[chunk(c)], s_d3.at[c], r_d3.at[c], dev_d)

    def c_d1(c):
        return rc(DS1.at[chunk(c)], DR0.at[chunk(c)], s_d1.at[c], r_d1.at[c], dev_d)

    def c_qz(i):
        return rc(QS.at[sub(i)], QR.at[sub(i)], s_qz.at[i], r_qz.at[i], dev_q)

    def c_lz(i):
        return rc(LS.at[sub(i)], LR.at[sub(i)], s_lz.at[i], r_lz.at[i], dev_l)

    def loop(lo, hi, body):
        def step(i, carry):
            body(i)
            return carry

        lax.fori_loop(lo, hi, step, 0)

    barrier = pltpu.get_barrier_semaphore()
    for dev in (dev_q, dev_l, dev_yf, dev_yb, dev_d, dev_qd):
        pl.semaphore_signal(barrier, inc=1, device_id=dev, device_id_type=MESH)
    in_q = pltpu.make_async_copy(q_ref, QB.at[0], s_in.at[0])
    in_l = pltpu.make_async_copy(l_ref, LB.at[0], s_in.at[1])
    in_q.start()
    in_l.start()
    in_q.wait()
    in_l.wait()
    pl.semaphore_wait(barrier, 6)

    def send_first(i):
        c_l(i).start()
        c_q(i).start()

        @pl.when(odd)
        def _():
            c_y(i).start()

    loop(0, ns, send_first)
    c_1().start()

    def slot_of(t):
        return jnp.where(t == 0, 0, jnp.where(t == 1, 2 - par, jnp.where(t == 2, 1, 2 * par)))

    def put(ts, k, cols, d):
        m = jnp.max(d, axis=0, keepdims=True)
        e = jnp.exp(d - m)
        E[ts, chunk(k), cols] = e
        MX[ts, pl.ds(k, 1), cols] = m
        SM[ts, pl.ds(k, 1), cols] = jnp.sum(e, axis=0, keepdims=True)

    def narrow_piece(s, k, c):
        for t in (2, 3):
            lab = LB[slot_of(t), chunk(k), :]
            d = lax.dot_general(lab, QB[2 + s, chunk(c), :], NT, preferred_element_type=F32) * factor
            put(2 * t + s, k, chunk(c), d)

    def wide(t, s, k):
        lab = LB[slot_of(t), chunk(k), :]
        d = lax.dot_general(lab, QB[2 * (t // 2) + s], NT, preferred_element_type=F32) * factor
        put(2 * t + s, k, slice(None), d)

        @pl.when((t == 0) & (s == 0))
        def _():
            row = lax.broadcasted_iota(jnp.int32, (CH, rows), 0) + k * CH
            col = lax.broadcasted_iota(jnp.int32, (CH, rows), 1)
            SII[pl.ds(k, 1), :] = jnp.sum(jnp.where(row == col, d, 0.0), axis=0, keepdims=True)

    ACC[...] = jnp.zeros_like(ACC)

    def phase1(x):
        k, j = x // 4, lax.rem(x, 4)

        @pl.when(k < nk)
        def _():
            c_l(x).wait_recv()

            @pl.when(even)
            def _():
                c_y(x).start()

            c_q(x).wait_recv()
            c_3(x).start()

        @pl.when((k == 0) & (j == 1))
        def _():
            c_1().wait_recv()

        @pl.when((k > 0) & (j < 2))
        def _():
            @pl.when(j == 1)
            def _():
                loop((k - 1) * per, k * per, lambda i: c_3(i).wait_recv())

            @pl.when((j == 0) & odd)
            def _():
                loop((k - 1) * per, k * per, lambda i: c_y(i).wait_recv())

            kk = k - 1
            m = jnp.where(k == nk, kk, 2 * kk + 1)
            loop(0, m, lambda i: narrow_piece(j, jnp.minimum(i, kk), jnp.where(i < kk, kk, i - kk)))

        @pl.when((k > 0) & (j == 2) & even)
        def _():
            loop((k - 1) * per, k * per, lambda i: c_y(i).wait_recv())

        lo = jnp.where(k == 0, jnp.where(j == 0, 0, j + 2), 0)
        cnt = jnp.where(
            k == 0, jnp.where(j == 0, 3, 1), jnp.where(j >= 2, 1, jnp.where(k == nk, 2, 0))
        )

        def piece(i):
            t = jnp.where(k == 0, 0, jnp.where(j >= 2, 1, 2 + i))
            s = jnp.where(k == 0, (lo + i) // 3, lax.rem(j, 2))
            kk = jnp.where(k == 0, lax.rem(lo + i, 3), k - 1)
            wide(t, s, kk)

        loop(0, cnt, piece)

    loop(0, 4 * (nk + 1), phase1)

    for s in range(4):
        p, h = s // 2, s % 2
        parts = [(2 * (2 * p + tt) + h, k) for tt in range(2) for k in range(nk)]
        m = functools.reduce(jnp.maximum, [MX[ts, k : k + 1, :] for ts, k in parts])
        total = sum(SM[ts, k : k + 1, :] * jnp.exp(MX[ts, k : k + 1, :] - m) for ts, k in parts)
        ST[s : s + 1, :] = m
        ST[4 + s : 5 + s, :] = total
    for j in range(3):
        c_st(j).start()
    for j in range(3):
        c_st(j).wait_recv()
    for s in range(4):
        p, h = s // 2, s % 2
        ms = [ST[s : s + 1, :]] + [RS[j, s ^ (j + 1) : (s ^ (j + 1)) + 1, :] for j in range(3)]
        ls = [ST[4 + s : 5 + s, :]] + [RS[j, 4 + (s ^ (j + 1)) : 5 + (s ^ (j + 1)), :] for j in range(3)]
        top = functools.reduce(jnp.maximum, ms)
        lse = top + jnp.log(sum(a * jnp.exp(b - top) for a, b in zip(ls, ms)))
        for tt in range(2):
            ts = 2 * (2 * p + tt) + h
            for k in range(nk):
                AL[ts, k : k + 1, :] = jnp.exp(MX[ts, k : k + 1, :] - lse)
        if s == 0:
            loss_ref[...] = lse - sum(SII[k : k + 1, :] for k in range(nk))

    def lg_piece(t, c):
        row = lax.broadcasted_iota(jnp.int32, (CH, rows), 0) + c * CH
        col = lax.broadcasted_iota(jnp.int32, (CH, rows), 1) + rows * jnp.minimum(t, 1)
        hit = jnp.where(row == col, 1.0, 0.0)
        w0 = (E[2 * t, chunk(c), :] * AL[2 * t, pl.ds(c, 1), :] - hit).astype(BF16)
        w1 = (E[2 * t + 1, chunk(c), :] * AL[2 * t + 1, pl.ds(c, 1), :]).astype(BF16)
        qs = 2 * (t // 2)
        g = lax.dot_general(w0, QB[qs], NN, preferred_element_type=F32)
        g = g + lax.dot_general(w1, QB[qs + 1], NN, preferred_element_type=F32)
        slot = slot_of(t)
        ACC[slot, chunk(c), :] = ACC[slot, chunk(c), :] + g

    def qg_piece(s, c):
        p, h = s // 2, lax.rem(s, 2)
        row = lax.broadcasted_iota(jnp.int32, (CH, CH), 0)
        col = lax.broadcasted_iota(jnp.int32, (CH, CH), 1) + c * CH + rows * jnp.minimum(s, 1)
        total = None
        for tt in range(2):
            t = 2 * p + tt
            ws = []
            for k in range(nk):
                x = E[2 * t + h, chunk(k), chunk(c)] * AL[2 * t + h, k : k + 1, chunk(c)]
                if tt == 0:
                    x = x - jnp.where(row + k * CH == col, 1.0, 0.0)
                ws.append(x.astype(BF16))
            g = lax.dot_general(jnp.concatenate(ws, axis=0), LB[slot_of(t)], TN, preferred_element_type=F32)
            total = g if total is None else total + g
        QGT[...] = total

    def service(i):
        c_yr(i).wait_recv()

        @pl.when(even)
        def _():
            LS[sub(i), :] = (ACC[1, sub(i), :] + YR[sub(i), :].astype(F32)).astype(BF16)
            c_lz(i).start()

    def phase3(x):
        first = x < 5 * nk
        y = x - 5 * nk
        c = jnp.where(first, x // 5, y // 3)
        v = jnp.where(first, lax.rem(x, 5), 5 + lax.rem(y + 3 * nk, 3))
        is_lg = (v == 0) | ((v >= 3) & (v <= 5))
        t = jnp.where(v == 0, 1 + 2 * par, jnp.where(v == 3, 2, jnp.where(v == 4, 3 - 2 * par, 0)))
        s = jnp.where(v == 1, 3, jnp.where(v == 2, 2, jnp.where(v == 6, 1, 0)))

        @pl.when(is_lg)
        def _():
            lg_piece(t, c)

        @pl.when(jnp.logical_not(is_lg))
        def _():
            qg_piece(s, c)

        @pl.when(v == 0)
        def _():
            YS[chunk(c), :] = ACC[2, chunk(c), :].astype(BF16)
            loop(c * per, (c + 1) * per, lambda i: c_yr(i).start())

        @pl.when(v == 1)
        def _():
            DS3[chunk(c), :] = QGT[...].astype(BF16)
            c_d3(c).start()

        @pl.when(v == 2)
        def _():
            c_d3(c).wait_recv()
            QS[chunk(c), :] = (QGT[...] + DR2[chunk(c), :].astype(F32)).astype(BF16)
            loop(c * per, (c + 1) * per, lambda i: c_qz(i).start())

        @pl.when((v == 4) & odd)
        def _():
            LS[chunk(c), :] = ACC[1, chunk(c), :].astype(BF16)
            loop(c * per, (c + 1) * per, lambda i: c_lz(i).start())

        @pl.when(v == 6)
        def _():
            DS1[chunk(c), :] = QGT[...].astype(BF16)
            c_d1(c).start()

        @pl.when(v == 7)
        def _():
            QG0[chunk(c), :] = QGT[...]

        @pl.when((x >= 5) & (lax.rem(x, 2) == 1))
        def _():
            service((x - 5) // 2)

    steps = 8 * nk
    loop(0, steps, phase3)
    loop((steps - 4) // 2, ns, service)
    loop(0, nk, lambda c: c_d1(c).wait_recv())

    def finish(i):
        c_qz(i).wait_recv()
        g = QG0[sub(i), :] + DR0[sub(i), :].astype(F32)
        QO[sub(i), :] = (g + QR[sub(i), :].astype(F32)).astype(BF16)
        pltpu.make_async_copy(QO.at[sub(i)], qg_ref.at[sub(i)], s_out.at[0]).start()
        c_lz(i).wait_recv()
        back = jnp.where(odd, YR[sub(i), :].astype(F32), 0.0)
        LO[sub(i), :] = (ACC[0, sub(i), :] + back + LR[sub(i), :].astype(F32)).astype(BF16)
        pltpu.make_async_copy(LO.at[sub(i)], lg_ref.at[sub(i)], s_out.at[1]).start()

    loop(0, ns, finish)

    def drain(i):
        for copy in (c_q, c_l, c_y, c_3, c_yr, c_qz, c_lz):
            copy(i).wait_send()

    loop(0, ns, drain)
    c_1().wait_send()
    for j in range(3):
        c_st(j).wait_send()

    def drain_cores(c):
        c_d3(c).wait_send()
        c_d1(c).wait_send()

    loop(0, nk, drain_cores)
    pltpu.make_async_copy(QO, qg_ref, s_out.at[0]).wait()
    pltpu.make_async_copy(LO, lg_ref, s_out.at[1]).wait()


def local(queries, labels, logit_scale):
    rows, width = queries.shape
    nk, ns = rows // CH, rows // SUB
    block = (rows, width)
    dma = pltpu.SemaphoreType.DMA
    loss, query_grad, label_grad = pl.pallas_call(
        kernel,
        out_shape=(
            jax.ShapeDtypeStruct((1, rows), F32),
            jax.ShapeDtypeStruct(block, BF16),
            jax.ShapeDtypeStruct(block, BF16),
        ),
        in_specs=[
            pl.BlockSpec(memory_space=pltpu.SMEM),
            pl.BlockSpec(memory_space=pl.ANY),
            pl.BlockSpec(memory_space=pl.ANY),
        ],
        out_specs=(
            pl.BlockSpec(memory_space=pltpu.VMEM),
            pl.BlockSpec(memory_space=pl.ANY),
            pl.BlockSpec(memory_space=pl.ANY),
        ),
        scratch_shapes=[
            pltpu.VMEM((4, *block), BF16),
            pltpu.VMEM((3, *block), BF16),
            pltpu.VMEM((8, rows, rows), F32),
            pltpu.VMEM((8, 8, rows), F32),
            pltpu.VMEM((8, 8, rows), F32),
            pltpu.VMEM((8, 8, rows), F32),
            pltpu.VMEM((8, rows), F32),
            pltpu.VMEM((3, 8, rows), F32),
            pltpu.VMEM((8, rows), F32),
            pltpu.VMEM((3, *block), F32),
            pltpu.VMEM((CH, width), F32),
            pltpu.VMEM(block, F32),
            *[pltpu.VMEM(block, BF16)] * 12,
            dma((2,)), dma((2,)),
            dma((ns,)), dma((ns,)),
            dma((ns,)), dma((ns,)),
            dma((ns,)), dma((ns,)),
            dma((1,)), dma((1,)),
            dma((ns,)), dma((ns,)),
            dma((3,)), dma((3,)),
            dma((ns,)), dma((ns,)),
            dma((nk,)), dma((nk,)),
            dma((ns,)), dma((ns,)),
            dma((ns,)), dma((ns,)),
            dma((nk,)), dma((nk,)),
        ],
        compiler_params=pltpu.CompilerParams(
            collective_id=0, has_side_effects=True, vmem_limit_bytes=62 * 2**20
        ),
        cost_estimate=pl.CostEstimate(
            flops=6 * rows * 8 * rows * width, bytes_accessed=8 * rows * width, transcendentals=8 * rows * rows
        ),
    )(logit_scale, queries, labels)
    return loss.reshape(rows), query_grad, label_grad


def solution(mesh):
    in_specs = (P(("wide", "narrow"), None), P(("wide", "narrow"), None), P())
    out_specs = (P(("wide", "narrow")), P(("wide", "narrow"), None), P(("wide", "narrow"), None))
    return jax.shard_map(local, mesh=mesh, in_specs=in_specs, out_specs=out_specs, check_vma=False)
```

time: 404 us -> 87.6 us (0.22)
  waiting for transfers between devices: 325 us -> 0 us
  Pallas kernels: 0 us -> 81.3 us
  matrix products: 37.2 us -> 0 us
  other arithmetic: 15.9 us -> 1.29 us
  between operations: 14.7 us -> 1.29 us
  local copies, waits for them, and re-layouts: 8.91 us -> 3.47 us
    ppermute x2 -> x0, waiting for transfers between devices: 206 us -> none  [from_behind(): return lax.ppermute(block, axis, route)]
    pallas_call x0 -> x1, Pallas kernels: none -> 81.3 us  [local(): pl.pallas_call(kernel, out_shape=(jax.ShapeDtypeStruct((1, rows), F32), j...]
    reduce_scatter x1 -> x0, waiting for transfers between devices: 71.9 us -> none  [local(): lax.psum_scatter(jnp.einsum('rc,rd->cd', picked, queries, preferred_eleme...]
    all_gather x1 -> x0, waiting for transfers between devices: 47 us -> none  [local(): own_labels = lax.all_gather(labels, 'narrow', axis=0, tiled=True)]
    dot_general x4 -> x0, matrix products: 37.2 us -> none  [the longest x1 13.7 us: local(): jnp.dot(weights, window, preferred_element_type=jnp.float32)]
    convert_element_type x2 -> x0, other arithmetic: 9.78 us -> none  [the longest x1 6.98 us: local(): (jnp.exp(scores - lse[:, None]) - hit.astype(jnp.float32)).astype(jnp.bfl...]
    reduce_sum x1 -> x0, other arithmetic: 5.51 us -> none  [local(): loss = lse - jnp.sum(jnp.where(hit, scores, 0.0), axis=1)]
  transfers between devices with their start and end apart: 4 -> 0, of which waited for: 4 -> 0; matrix products, arithmetic and copies ran while one was open for 4% -> 0% of each run, Pallas kernels for 0% -> 0%
where the time goes in v1:
time: 87.6 us; the launch traced here: 87.4 us
  Pallas kernels  81.3 us (93%)
  local copies, waits for them, and re-layouts  3.47 us (4%)
  other arithmetic  1.29 us (1%)
  between operations  1.29 us (1%)
    pallas_call x1, Pallas kernels, local(): pl.pallas_call(kernel, out_shape=(jax.ShapeDtypeStruct((1, rows), F32), j...  81.3 us
    unnamed x4, local copies, waits for them, and re-layouts  3.47 us

profile of v1, /device:TPU:1, one launch (start us, length us, event | category | flops | bytes accessed | tf_op | source)
XLA Modules:
  0.0 87.4 jit_solution(15570879394822786055)
XLA Ops:
  1.3 81.3 %shard_map.58 = (f32[1,768]{1,0:T(1,128)}, bf16[768,768]{1,0:T(8,128)(2,1)}, bf16[768,768]{1,0:T(8,128)(2,1)}) custom-call(f32[1]{0:T(128)S(6)} %copy.8.scale_ref, bf16[768,768]{1,0:T(8,128)(2,1)} %q_ref.1, bf16[768,768]{1,0:T(8,128)(2,1)} %l_ref.1), custom_call_target="tpu_custom_call" | custom-call | flops 21743271936 | bytes 4718592 | tf_op jit(solution)/shard_map/pallas_call | solution.py:346
  82.6 1.3 %reduce = f32[768]{0:T(1024)} reduce(f32[1,768]{1,0:T(1,128)} %get-tuple-element.6, f32[]{:T(128)} %constant), dimensions={0}, to_apply=%get-tuple-element.6.reduce_sub_computation | reduce | bytes 6148 | tf_op jit(solution)/shard_map/pallas_call | solution.py:346
  83.9 0.0 copy-start
  83.9 2.5 %copy.9 = bf16[768,768]{1,0:T(8,128)(2,1)} copy(bf16[768,768]{1,0:T(8,128)(2,1)} %get-tuple-element.13) | data formatting | bytes 2359296
  86.3 0.0 copy-done
  86.3 1.0 %copy.10 = bf16[768,768]{1,0:T(8,128)(2,1)} copy(bf16[768,768]{1,0:T(8,128)(2,1)S(1)} %copy-done) | data formatting | bytes 2359296
Async XLA Ops:
  83.9 2.5 %copy-start = (bf16[768,768]{1,0:T(8,128)(2,1)S(1)}, bf16[768,768]{1,0:T(8,128)(2,1)}, u32[]{:S(2)}) copy-start(bf16[768,768]{1,0:T(8,128)(2,1)} %get-tuple-element.14) | copy-start | bytes 3538948

commit v2 on v0

v2 whole, which is shorter than its diff:
```python
import functools
import math

import jax
import jax.numpy as jnp
from jax import lax
from jax.experimental import pallas as pl
from jax.experimental.pallas import tpu as pltpu
from jax.sharding import PartitionSpec as P

MESH = pl.DeviceIdType.MESH
F32, BF16 = jnp.float32, jnp.bfloat16
CH = 256
SUB = 64
NT = (((1,), (1,)), ((), ()))
NN = (((1,), (0,)), ((), ()))
TN = (((0,), (0,)), ((), ()))
OWN_Q, GOT_Q, PASSED, OWN_L, GOT_L = 0, 2, 4, 6, 7


def kernel(
    scale_ref, q_ref, l_ref, loss_ref, qg_ref, lg_ref,
    B, E, MX, SM, AL, SA, SB, RA, RB, SII, TR, ACC, QG0, GT,
    YS, LS, QS, DS3, DS5, DS1, YR, LR, QR, DR2, DR4, DR0,
    s_in, s_q, r_q, s_l, r_l, s_y, r_y, s_1, r_1, s_3, r_3, s_5, r_5, s_sa, r_sa, s_sb, r_sb,
    s_yr, r_yr, s_qz, r_qz, s_lz, r_lz, s_d3, r_d3, s_d5, r_d5, s_d1, r_d1,
):
    rows = q_ref.shape[0]
    nk, ns = rows // CH, rows // SUB
    per = CH // SUB
    w, n = lax.axis_index("wide"), lax.axis_index("narrow")
    nw = lax.axis_size("wide")
    par = lax.rem(w, 2)
    even, odd = par == 0, par == 1
    wx = w + 1 - 2 * par
    nc = n + 1 - 2 * lax.rem(n, 2)

    def at(step):
        return lax.rem(w + nw + step, nw)

    dev_q, dev_l = (wx, n), (wx, lax.rem(n + 2, 4))
    dev_d, dev_qd = (w, nc), (wx, nc)
    out_y = (at(4 * par - 2), n)
    back_y = (at(2 - 4 * par), n)
    factor = scale_ref[0] * (1.0 / math.sqrt(q_ref.shape[1]))

    def sub(i):
        return pl.ds(pl.multiple_of(i * SUB, SUB), SUB)

    def chunk(c):
        return pl.ds(pl.multiple_of(c * CH, CH), CH)

    def rc(src, dst, ssem, rsem, dev):
        return pltpu.make_async_remote_copy(
            src_ref=src, dst_ref=dst, send_sem=ssem, recv_sem=rsem, device_id=dev, device_id_type=MESH
        )

    def c_q(i):
        return rc(q_ref.at[sub(i)], B.at[GOT_Q, sub(i)], s_q.at[i], r_q.at[i], dev_q)

    def c_l(i):
        return rc(l_ref.at[sub(i)], B.at[GOT_L, sub(i)], s_l.at[i], r_l.at[i], dev_l)

    def c_y(i):
        return rc(B.at[OWN_L * par, sub(i)], B.at[PASSED, sub(i)], s_y.at[i], r_y.at[i], out_y)

    def c_1():
        return rc(q_ref, B.at[OWN_Q + 1], s_1.at[0], r_1.at[0], dev_d)

    def c_3(i):
        return rc(B.at[GOT_Q, sub(i)], B.at[GOT_Q + 1, sub(i)], s_3.at[i], r_3.at[i], dev_d)

    def c_5(i):
        return rc(B.at[PASSED, sub(i)], B.at[PASSED + 1, sub(i)], s_5.at[i], r_5.at[i], dev_d)

    def c_sa(j, dev):
        return rc(SA, RA.at[j], s_sa.at[j], r_sa.at[j], dev)

    def c_sb(i, j, dev):
        return rc(SB, RB.at[j], s_sb.at[i], r_sb.at[j], dev)

    def c_yr(i):
        return rc(YS.at[sub(i)], YR.at[sub(i)], s_yr.at[i], r_yr.at[i], back_y)

    def c_qz(i):
        return rc(QS.at[sub(i)], QR.at[sub(i)], s_qz.at[i], r_qz.at[i], dev_q)

    def c_lz(i):
        return rc(LS.at[sub(i)], LR.at[sub(i)], s_lz.at[i], r_lz.at[i], dev_l)

    def c_d3(c):
        return rc(DS3.at[chunk(c)], DR2.at[chunk(c)], s_d3.at[c], r_d3.at[c], dev_d)

    def c_d5(c):
        return rc(DS5.at[chunk(c)], DR4.at[chunk(c)], s_d5.at[c], r_d5.at[c], dev_d)

    def c_d1(c):
        return rc(DS1.at[chunk(c)], DR0.at[chunk(c)], s_d1.at[c], r_d1.at[c], dev_d)

    def loop(lo, hi, body):
        def step(i, carry):
            body(i)
            return carry

        lax.fori_loop(lo, hi, step, 0)

    in_q = pltpu.make_async_copy(q_ref, B.at[OWN_Q], s_in.at[0])
    in_l = pltpu.make_async_copy(l_ref, B.at[OWN_L], s_in.at[1])
    in_q.start()
    in_l.start()
    barrier = pltpu.get_barrier_semaphore()
    for dev in (back_y, out_y, dev_l, dev_q, dev_qd, dev_d):
        pl.semaphore_signal(barrier, inc=1, device_id=dev, device_id_type=MESH)
    in_q.wait()
    in_l.wait()
    pl.semaphore_wait(barrier, 6)

    def send_first(i):
        c_y(i).start()
        c_l(i).start()
        c_q(i).start()

    loop(0, ns, send_first)
    c_1().start()

    def labels_of(t):
        return jnp.where(t == 0, OWN_L, jnp.where(t == 3, OWN_L - 2 * par, GOT_L))

    def queries_of(t):
        return jnp.where(t == 0, OWN_Q, jnp.where(t == 1, PASSED - PASSED * par, GOT_Q))

    def scores(t, h, row0, height, col0, width):
        lab = B[labels_of(t), pl.ds(row0, height), :]
        qry = B[queries_of(t) + h, pl.ds(col0, width), :]
        return lax.dot_general(lab, qry, NT, preferred_element_type=F32) * factor

    def put(ts, k, cols, d):
        m = jnp.max(d, axis=0, keepdims=True)
        e = jnp.exp(d - m)
        E[ts, chunk(k), cols] = e
        MX[k, pl.ds(ts, 1), cols] = m
        SM[k, pl.ds(ts, 1), cols] = jnp.sum(e, axis=0, keepdims=True)

    def own_piece(h, k):
        d = scores(0, h, pl.multiple_of(k * CH, CH), CH, 0, rows)
        put(h, k, slice(None), d)

        @pl.when(h == 0)
        def _():
            row = lax.broadcasted_iota(jnp.int32, (CH, rows), 0) + k * CH
            col = lax.broadcasted_iota(jnp.int32, (CH, rows), 1)
            SII[pl.ds(k, 1), :] = jnp.sum(jnp.where(row == col, d, 0.0), axis=0, keepdims=True)

    def square_piece(h, k, c):
        for t in (1, 2, 3):
            d = scores(t, h, pl.multiple_of(k * CH, CH), CH, pl.multiple_of(c * CH, CH), CH)
            put(2 * t + h, k, chunk(c), d)

    def take_in(i):
        c_q(i).wait_recv()
        c_3(i).start()
        c_y(i).wait_recv()

        @pl.when(even)
        def _():
            c_5(i).start()

    def arrived(lo, hi):
        loop(lo, hi, lambda i: c_3(i).wait_recv())

        @pl.when(even)
        def _():
            loop(lo, hi, lambda i: c_5(i).wait_recv())

    def phase1(x):
        k, j = x // 8, lax.rem(x, 8)
        i, h, kk = lax.rem(j, 3), j // 3, k - 1
        loop(x * per // 8, (x + 1) * per // 8, take_in)

        @pl.when((k == 0) & (j == 3))
        def _():
            c_1().wait_recv()

        @pl.when((k == 0) & (j < 6))
        def _():
            own_piece(h, i)

        @pl.when((k > 0) & (j == 0))
        def _():
            loop(kk * per, k * per, lambda i: c_l(i).wait_recv())

        @pl.when((k > 0) & (j == 3))
        def _():
            arrived(kk * per, k * per)

        @pl.when((k > 0) & (j < 6) & (i < 2 * kk + 1))
        def _():
            square_piece(h, jnp.minimum(i, kk), jnp.where(i < kk, kk, i - kk))

    loop(0, 8 * nk, phase1)
    loop((nk - 1) * per, ns, lambda i: c_l(i).wait_recv())
    edge = (nk - 1) * CH

    def last_pieces(h):
        @pl.when(h == 1)
        def _():
            arrived((nk - 1) * per, ns)

        for t in (1, 2, 3):
            d = scores(t, h, 0, rows, edge, CH)
            for k in range(nk):
                put(2 * t + h, k, slice(edge, rows), d[k * CH : (k + 1) * CH])
        for t in (1, 2, 3):
            put(2 * t + h, nk - 1, slice(0, edge), scores(t, h, edge, CH, 0, edge))

    loop(0, 2, last_pieces)

    def lg_piece(t0, count, c):
        def term(i):
            t = t0 + i
            row = lax.broadcasted_iota(jnp.int32, (CH, rows), 0) + c * CH
            col = lax.broadcasted_iota(jnp.int32, (CH, rows), 1) + rows * jnp.minimum(t, 1)
            hit = jnp.where(row == col, 1.0, 0.0)
            w0 = (E[2 * t, chunk(c), :] * AL[c, pl.ds(2 * t, 1), :] - hit).astype(BF16)
            w1 = (E[2 * t + 1, chunk(c), :] * AL[c, pl.ds(2 * t + 1, 1), :]).astype(BF16)
            g = lax.dot_general(w0, B[queries_of(t)], NN, preferred_element_type=F32)
            g = g + lax.dot_general(w1, B[queries_of(t) + 1], NN, preferred_element_type=F32)

            @pl.when(i == 0)
            def _():
                GT[...] = g

            @pl.when(i > 0)
            def _():
                GT[...] = GT[...] + g

        loop(0, count, term)

    def qg_piece(t0, count, h, c):
        def term(i):
            t = t0 + i
            ts = 2 * t + h
            row = lax.broadcasted_iota(jnp.int32, (CH, CH), 0)
            col = lax.broadcasted_iota(jnp.int32, (CH, CH), 1) + c * CH + rows * jnp.minimum(ts, 1)
            ws = []
            for k in range(nk):
                x = E[ts, chunk(k), chunk(c)] * AL[k, pl.ds(ts, 1), chunk(c)]
                ws.append((x - jnp.where(row + k * CH == col, 1.0, 0.0)).astype(BF16))
            g = lax.dot_general(
                jnp.concatenate(ws, axis=0), B[labels_of(t)], TN, preferred_element_type=F32
            )

            @pl.when(i == 0)
            def _():
                GT[...] = g

            @pl.when(i > 0)
            def _():
                GT[...] = GT[...] + g

        loop(0, count, term)

    def join(*parts):
        top = functools.reduce(jnp.maximum, parts)
        return top + jnp.log(sum(jnp.exp(part - top) for part in parts))

    m = functools.reduce(jnp.maximum, [MX[k] for k in range(nk)])
    of_term = m + jnp.log(sum(SM[k] * jnp.exp(MX[k] - m) for k in range(nk)))
    third = of_term[2:4]
    SA[0:2, :] = jnp.where(odd, join(of_term[0:2], third), of_term[0:2])
    SA[2:4, :] = join(of_term[4:6], of_term[6:8])
    SB[...] = third

    def near():
        return [c_sa(0, dev_d), c_sa(1, dev_q), c_sa(2, dev_qd)]

    def far_even():
        return [
            c_sb(1, 1, (at(3), n)), c_sb(2, 2, (at(3), nc)), c_sb(3, 1, (at(2), n)), c_sb(4, 2, (at(2), nc)),
            c_sa(5, (at(-2), n)), c_sa(6, (at(-2), nc)), c_sb(0, 0, dev_d),
        ]

    def far_odd():
        return [c_sa(3, (at(-3), n)), c_sa(4, (at(-3), nc))]

    def each(copies, act):
        for copy in copies:
            act(copy)

    pl.when(even)(lambda: each(far_even(), lambda copy: copy.start()))
    pl.when(odd)(lambda: each(far_odd(), lambda copy: copy.start()))
    each(near(), lambda copy: copy.start())

    got = SA[2:4, :]
    own_view = jnp.concatenate([of_term[0:4], got, got], axis=0)
    for k in range(nk):
        AL[k] = jnp.exp(MX[k] - own_view)

    def early(i):
        of_got = lax.rem(i, 2) == 0

        @pl.when(of_got | even)
        def _():
            qg_piece(jnp.where(of_got, 2, 1), jnp.where(of_got, 2, 1), 1 - i // 2, 0)

        @pl.when(i == 0)
        def _():
            DS3[:CH, :] = GT[...].astype(BF16)
            c_d3(0).start()

        @pl.when((i == 1) & even)
        def _():
            DS5[:CH, :] = GT[...].astype(BF16)
            c_d5(0).start()

        @pl.when((i == 2) | ((i == 3) & even))
        def _():
            QG0[chunk(i - 2), :] = GT[...]

    loop(0, 4, early)

    def swap(x):
        return jnp.concatenate([x[1:2], x[0:1]], axis=0)

    each(near(), lambda copy: copy.wait_recv())
    for j in (1, 2):
        c_sb(j, j, dev_d).wait_recv()

    @pl.when(even)
    def _():
        for j in (3, 4, 5, 6):
            c_sa(j, dev_d).wait_recv()
        c_sb(0, 0, dev_d).wait_recv()

    far = [RB[1], swap(RB[2])]
    near0 = [SA[0:2, :], swap(RA[0, 0:2, :]), RA[1, 2:4, :], swap(RA[2, 2:4, :])]
    near1 = [SA[2:4, :], swap(RA[0, 2:4, :]), RA[1, 0:2, :], swap(RA[2, 0:2, :])]

    def settle(lse0, lse1, lse2):
        lse = jnp.concatenate([lse0, lse2, lse1, lse1], axis=0)
        for k in range(nk):
            AL[k] = jnp.exp(MX[k] - lse)
        loss_ref[...] = lse0[0:1] - sum(SII[k : k + 1, :] for k in range(nk))
        TR[0:1, :] = jnp.exp(SA[2:3, :CH] - lse1[0:1, :CH])
        TR[1:2, :] = jnp.exp(RA[0, 3:4, :CH] - lse1[0:1, :CH])
        TR[2:3, :] = jnp.exp(SB[0:1, :CH] - lse2[0:1, :CH])

    @pl.when(even)
    def _():
        of_passed = [SB[...], swap(RB[0]), RA[5, 0:2, :], swap(RA[6, 0:2, :]), RA[3, 2:4, :], swap(RA[4, 2:4, :])]
        lse2 = join(*of_passed)
        settle(join(*near0, *far), join(*near1), lse2)
        TR[3:4, :] = jnp.exp(RB[0, 1:2, :CH] - lse2[0:1, :CH])

    @pl.when(odd)
    def _():
        lse0 = join(*near0)
        settle(lse0, join(*near1, *far), lse0)

    def send(copy, c):
        loop(c * per, (c + 1) * per, lambda i: copy(i).start())

    column = jnp.transpose(TR[...])
    c_d3(0).wait_recv()
    QS[:CH, :] = (QG0[:CH, :] * column[:, 0:1] + DR2[:CH, :].astype(F32) * column[:, 1:2]).astype(BF16)
    send(c_qz, 0)

    @pl.when(even)
    def _():
        c_d5(0).wait_recv()
        g = QG0[CH : 2 * CH, :] * column[:, 2:3] + DR4[:CH, :].astype(F32) * column[:, 3:4]
        YS[:CH, :] = g.astype(BF16)
        send(c_yr, 0)

    def phase3(x):
        first = x < 5 * nk
        y = x - 5 * nk
        c = jnp.where(first, x // 5, y // 4)
        v = jnp.where(first, lax.rem(x, 5), 6 + lax.rem(y + 8 * nk, 4))
        lg = (v == 2) | (v == 7) | ((v == 1) & odd) | ((v == 8) & even)
        later = (c > 0) | (v >= 6)
        qg = later & ((v == 0) | (v == 3) | (v == 6) | (v == 9) | (((v == 1) | (v == 4)) & even))

        @pl.when(lg)
        def _():
            t0 = jnp.where(v == 2, 1, jnp.where(v == 7, 0, 3))
            lg_piece(t0, jnp.where(v == 2, 2, 1), c)

        @pl.when(qg)
        def _():
            passed = (v == 1) | (v == 4)
            t0 = jnp.where(passed, 1, jnp.where(v >= 6, 0, 2))
            count = jnp.where(passed, 1, jnp.where(v >= 6, 1 + par, 2))
            qg_piece(t0, count, jnp.where((v == 0) | (v == 1) | (v == 6), 1, 0), c)

        @pl.when((v == 0) & later)
        def _():
            DS3[chunk(c), :] = GT[...].astype(BF16)
            c_d3(c).start()

        @pl.when((v == 1) & even & later)
        def _():
            DS5[chunk(c), :] = GT[...].astype(BF16)
            c_d5(c).start()

        @pl.when((v == 1) & odd)
        def _():
            YS[chunk(c), :] = GT[...].astype(BF16)
            send(c_yr, c)

        @pl.when(v == 2)
        def _():
            LS[chunk(c), :] = GT[...].astype(BF16)
            send(c_lz, c)

        @pl.when((v == 3) & later)
        def _():
            c_d3(c).wait_recv()
            QS[chunk(c), :] = (GT[...] + DR2[chunk(c), :].astype(F32)).astype(BF16)
            send(c_qz, c)

        @pl.when((v == 4) & even & later)
        def _():
            c_d5(c).wait_recv()
            YS[chunk(c), :] = (GT[...] + DR4[chunk(c), :].astype(F32)).astype(BF16)
            send(c_yr, c)

        @pl.when(v == 6)
        def _():
            DS1[chunk(c), :] = GT[...].astype(BF16)
            c_d1(c).start()

        @pl.when(v == 7)
        def _():
            ACC[chunk(c), :] = GT[...]

        @pl.when((v == 8) & even)
        def _():
            ACC[chunk(c), :] = ACC[chunk(c), :] + GT[...]

        @pl.when(v == 9)
        def _():
            QG0[chunk(c), :] = GT[...]

    loop(0, 9 * nk, phase3)
    loop(0, nk, lambda c: c_d1(c).wait_recv())

    def finish(i):
        c_yr(i).wait_recv()
        passed = YR[sub(i), :].astype(F32)
        c_qz(i).wait_recv()
        g = QG0[sub(i), :] + DR0[sub(i), :].astype(F32) + jnp.where(even, passed, 0.0)
        qg_ref[sub(i), :] = (g + QR[sub(i), :].astype(F32)).astype(BF16)
        c_lz(i).wait_recv()
        g = ACC[sub(i), :] + jnp.where(odd, passed, 0.0)
        lg_ref[sub(i), :] = (g + LR[sub(i), :].astype(F32)).astype(BF16)

    loop(0, ns, finish)

    def drain(i):
        for copy in (c_q, c_l, c_y, c_3, c_yr, c_qz, c_lz):
            copy(i).wait_send()

        @pl.when(even)
        def _():
            c_5(i).wait_send()

    loop(0, ns, drain)
    c_1().wait_send()
    each(near(), lambda copy: copy.wait_send())
    pl.when(even)(lambda: each(far_even(), lambda copy: copy.wait_send()))
    pl.when(odd)(lambda: each(far_odd(), lambda copy: copy.wait_send()))

    def drain_cores(c):
        c_d3(c).wait_send()
        c_d1(c).wait_send()

        @pl.when(even)
        def _():
            c_d5(c).wait_send()

    loop(0, nk, drain_cores)


def local(queries, labels, logit_scale):
    rows, width = queries.shape
    nk, ns = rows // CH, rows // SUB
    block = (rows, width)
    dma = pltpu.SemaphoreType.DMA
    counts = [ns, ns, ns, 1, ns, ns, 7, 5, ns, ns, ns, nk, nk, nk]
    loss, query_grad, label_grad = pl.pallas_call(
        kernel,
        out_shape=(
            jax.ShapeDtypeStruct((1, rows), F32),
            jax.ShapeDtypeStruct(block, BF16),
            jax.ShapeDtypeStruct(block, BF16),
        ),
        in_specs=[
            pl.BlockSpec(memory_space=pltpu.SMEM),
            pl.BlockSpec(memory_space=pltpu.HBM),
            pl.BlockSpec(memory_space=pltpu.HBM),
        ],
        out_specs=(pl.BlockSpec(memory_space=pltpu.VMEM),) * 3,
        scratch_shapes=[
            pltpu.VMEM((8, *block), BF16),
            pltpu.VMEM((8, rows, rows), F32),
            pltpu.VMEM((nk, 8, rows), F32),
            pltpu.VMEM((nk, 8, rows), F32),
            pltpu.VMEM((nk, 8, rows), F32),
            pltpu.VMEM((4, rows), F32),
            pltpu.VMEM((2, rows), F32),
            pltpu.VMEM((7, 4, rows), F32),
            pltpu.VMEM((3, 2, rows), F32),
            pltpu.VMEM((8, rows), F32),
            pltpu.VMEM((8, CH), F32),
            pltpu.VMEM(block, F32),
            pltpu.VMEM(block, F32),
            pltpu.VMEM((CH, width), F32),
            *[pltpu.VMEM(block, BF16)] * 12,
            dma((2,)),
            *[dma((count,)) for count in counts for _ in range(2)],
        ],
        compiler_params=pltpu.CompilerParams(
            collective_id=0, has_side_effects=True, vmem_limit_bytes=51 * 2**20
        ),
        cost_estimate=pl.CostEstimate(
            flops=6 * rows * 8 * rows * width, bytes_accessed=8 * rows * width, transcendentals=8 * rows * rows
        ),
    )(logit_scale, queries, labels)
    return loss.reshape(rows), query_grad, label_grad


def solution(mesh):
    in_specs = (P(("wide", "narrow"), None), P(("wide", "narrow"), None), P())
    out_specs = (P(("wide", "narrow")), P(("wide", "narrow"), None), P(("wide", "narrow"), None))
    return jax.shard_map(local, mesh=mesh, in_specs=in_specs, out_specs=out_specs, check_vma=False)
```

time: 404 us -> 82.4 us (0.20)
  waiting for transfers between devices: 325 us -> 0 us
  Pallas kernels: 0 us -> 78.3 us
  matrix products: 37.2 us -> 0 us
  other arithmetic: 15.9 us -> 0.61 us
  between operations: 14.7 us -> 1.29 us
  local copies, waits for them, and re-layouts: 8.91 us -> 2.03 us
    ppermute x2 -> x0, waiting for transfers between devices: 206 us -> none  [from_behind(): return lax.ppermute(block, axis, route)]
    pallas_call x0 -> x1, Pallas kernels: none -> 78.3 us  [local(): pl.pallas_call(kernel, out_shape=(jax.ShapeDtypeStruct((1, rows), F32), j...]
    reduce_scatter x1 -> x0, waiting for transfers between devices: 71.9 us -> none  [local(): lax.psum_scatter(jnp.einsum('rc,rd->cd', picked, queries, preferred_eleme...]
    all_gather x1 -> x0, waiting for transfers between devices: 47 us -> none  [local(): own_labels = lax.all_gather(labels, 'narrow', axis=0, tiled=True)]
    dot_general x4 -> x0, matrix products: 37.2 us -> none  [the longest x1 13.7 us: local(): jnp.dot(weights, window, preferred_element_type=jnp.float32)]
    convert_element_type x2 -> x0, other arithmetic: 9.78 us -> none  [the longest x1 6.98 us: local(): (jnp.exp(scores - lse[:, None]) - hit.astype(jnp.float32)).astype(jnp.bfl...]
    reduce_sum x1 -> x0, other arithmetic: 5.51 us -> none  [local(): loss = lse - jnp.sum(jnp.where(hit, scores, 0.0), axis=1)]
    unnamed x7 -> x2, local copies, waits for them, and re-layouts: 6.27 us -> 2.03 us
  transfers between devices with their start and end apart: 4 -> 0, of which waited for: 4 -> 0; matrix products, arithmetic and copies ran while one was open for 4% -> 0% of each run, Pallas kernels for 0% -> 0%
where the time goes in v2:
time: 82.4 us; the launch traced here: 82.2 us
  Pallas kernels  78.3 us (95%)
  local copies, waits for them, and re-layouts  2.03 us (2%)
  between operations  1.29 us (2%)
    pallas_call x1, Pallas kernels, local(): pl.pallas_call(kernel, out_shape=(jax.ShapeDtypeStruct((1, rows), F32), j...  78.3 us
    unnamed x2, local copies, waits for them, and re-layouts  2.03 us

profile of v2, /device:TPU:1, one launch (start us, length us, event | category | flops | bytes accessed | tf_op | source)
XLA Modules:
  0.0 82.2 jit_solution(4927060925929782520)
XLA Ops:
  1.3 78.3 %shard_map.58 = (f32[1,768]{1,0:T(1,128)S(1)}, bf16[768,768]{1,0:T(8,128)(2,1)S(1)}, bf16[768,768]{1,0:T(8,128)(2,1)S(1)}) custom-call(f32[1]{0:T(128)S(6)} %copy.8.scale_ref, bf16[768,768]{1,0:T(8,128)(2,1)} %q_ref.1, bf16[768,768]{1,0:T(8,128)(2,1)} %l_ref.1), custom_call_target="tpu_custom_call" | custom-call | flops 21743271936 | bytes 4718592 | tf_op jit(solution)/shard_map/pallas_call | solution.py:491
  79.6 0.6 reduce
  80.2 1.0 %copy.9 = bf16[768,768]{1,0:T(8,128)(2,1)} copy(bf16[768,768]{1,0:T(8,128)(2,1)S(1)} %get-tuple-element.13) | data formatting | bytes 2359296
  81.2 1.0 %copy.10 = bf16[768,768]{1,0:T(8,128)(2,1)} copy(bf16[768,768]{1,0:T(8,128)(2,1)S(1)} %get-tuple-element.14) | data formatting | bytes 2359296

commit v3 on v2

--- a/solution.py
+++ b/solution.py
@@ -11,7 +11,7 @@
 MESH = pl.DeviceIdType.MESH
 F32, BF16 = jnp.float32, jnp.bfloat16
 CH = 256
-SUB = 64
+SUB = 128
 NT = (((1,), (1,)), ((), ()))
 NN = (((1,), (0,)), ((), ()))
 TN = (((0,), (0,)), ((), ()))
@@ -198,24 +198,26 @@
             square_piece(h, jnp.minimum(i, kk), jnp.where(i < kk, kk, i - kk))
 
     loop(0, 8 * nk, phase1)
+    edge = (nk - 1) * CH
+
+    def last_queries(h, upto):
+        for t in (1, 2, 3):
+            d = scores(t, h, 0, upto, edge, CH)
+            for k in range(upto // CH):
+                put(2 * t + h, k, slice(edge, rows), d[k * CH : (k + 1) * CH])
+
+    def last_labels(h, upto):
+        for t in (1, 2, 3):
+            put(2 * t + h, nk - 1, slice(0, upto), scores(t, h, edge, CH, 0, upto))
+
+    last_queries(0, edge)
     loop((nk - 1) * per, ns, lambda i: c_l(i).wait_recv())
-    edge = (nk - 1) * CH
-
-    def last_pieces(h):
-        @pl.when(h == 1)
-        def _():
-            arrived((nk - 1) * per, ns)
-
-        for t in (1, 2, 3):
-            d = scores(t, h, 0, rows, edge, CH)
-            for k in range(nk):
-                put(2 * t + h, k, slice(edge, rows), d[k * CH : (k + 1) * CH])
-        for t in (1, 2, 3):
-            put(2 * t + h, nk - 1, slice(0, edge), scores(t, h, edge, CH, 0, edge))
-
-    loop(0, 2, last_pieces)
-
-    def lg_piece(t0, count, c):
+    last_labels(0, rows)
+    last_labels(1, edge)
+    arrived((nk - 1) * per, ns)
+    last_queries(1, rows)
+
+    def lg_piece(t0, count, c, more=False):
         def term(i):
             t = t0 + i
             row = lax.broadcasted_iota(jnp.int32, (CH, rows), 0) + c * CH
@@ -225,6 +227,9 @@
             w1 = (E[2 * t + 1, chunk(c), :] * AL[c, pl.ds(2 * t + 1, 1), :]).astype(BF16)
             g = lax.dot_general(w0, B[queries_of(t)], NN, preferred_element_type=F32)
             g = g + lax.dot_general(w1, B[queries_of(t) + 1], NN, preferred_element_type=F32)
+            if more:
+                GT[...] = GT[...] + g
+                return
 
             @pl.when(i == 0)
             def _():
@@ -322,44 +327,61 @@
     def swap(x):
         return jnp.concatenate([x[1:2], x[0:1]], axis=0)
 
+    def settle(first, pairs):
+        lse = jnp.concatenate(pairs, axis=0)
+        last = first + lse.shape[0]
+        for k in range(nk):
+            AL[k, first:last, :] = jnp.exp(MX[k, first:last, :] - lse)
+
+    def send(copy, c):
+        loop(c * per, (c + 1) * per, lambda i: copy(i).start())
+
     each(near(), lambda copy: copy.wait_recv())
+    near0 = [SA[0:2, :], swap(RA[0, 0:2, :]), RA[1, 2:4, :], swap(RA[2, 2:4, :])]
+    near1 = [SA[2:4, :], swap(RA[0, 2:4, :]), RA[1, 0:2, :], swap(RA[2, 0:2, :])]
+
+    @pl.when(even)
+    def _():
+        lse1 = join(*near1)
+        settle(4, [lse1, lse1])
+        TR[4:6, :] = lse1[:, :CH]
+
+    @pl.when(odd)
+    def _():
+        lse0 = join(*near0)
+        settle(0, [lse0, lse0])
+        loss_ref[...] = (lse0[0:1] - sum(SII[k : k + 1, :] for k in range(nk))).reshape(rows)
+
+    lg_piece(2 - par, 1, 0)
+
     for j in (1, 2):
         c_sb(j, j, dev_d).wait_recv()
+    far = [RB[1], swap(RB[2])]
 
     @pl.when(even)
     def _():
         for j in (3, 4, 5, 6):
             c_sa(j, dev_d).wait_recv()
         c_sb(0, 0, dev_d).wait_recv()
-
-    far = [RB[1], swap(RB[2])]
-    near0 = [SA[0:2, :], swap(RA[0, 0:2, :]), RA[1, 2:4, :], swap(RA[2, 2:4, :])]
-    near1 = [SA[2:4, :], swap(RA[0, 2:4, :]), RA[1, 0:2, :], swap(RA[2, 0:2, :])]
-
-    def settle(lse0, lse1, lse2):
-        lse = jnp.concatenate([lse0, lse2, lse1, lse1], axis=0)
-        for k in range(nk):
-            AL[k] = jnp.exp(MX[k] - lse)
-        loss_ref[...] = lse0[0:1] - sum(SII[k : k + 1, :] for k in range(nk))
-        TR[0:1, :] = jnp.exp(SA[2:3, :CH] - lse1[0:1, :CH])
-        TR[1:2, :] = jnp.exp(RA[0, 3:4, :CH] - lse1[0:1, :CH])
+        lse0 = join(*near0, *far)
+        lse2 = join(SB[...], swap(RB[0]), RA[5, 0:2, :], swap(RA[6, 0:2, :]), RA[3, 2:4, :], swap(RA[4, 2:4, :]))
+        settle(0, [lse0, lse2])
+        loss_ref[...] = (lse0[0:1] - sum(SII[k : k + 1, :] for k in range(nk))).reshape(rows)
         TR[2:3, :] = jnp.exp(SB[0:1, :CH] - lse2[0:1, :CH])
-
-    @pl.when(even)
-    def _():
-        of_passed = [SB[...], swap(RB[0]), RA[5, 0:2, :], swap(RA[6, 0:2, :]), RA[3, 2:4, :], swap(RA[4, 2:4, :])]
-        lse2 = join(*of_passed)
-        settle(join(*near0, *far), join(*near1), lse2)
         TR[3:4, :] = jnp.exp(RB[0, 1:2, :CH] - lse2[0:1, :CH])
 
     @pl.when(odd)
     def _():
-        lse0 = join(*near0)
-        settle(lse0, join(*near1, *far), lse0)
-
-    def send(copy, c):
-        loop(c * per, (c + 1) * per, lambda i: copy(i).start())
-
+        lse1 = join(*near1, *far)
+        settle(4, [lse1, lse1])
+        TR[4:6, :] = lse1[:, :CH]
+
+    lg_piece(1 + par, 1, 0, more=True)
+    LS[:CH, :] = GT[...].astype(BF16)
+    send(c_lz, 0)
+
+    TR[0:1, :] = jnp.exp(SA[2:3, :CH] - TR[4:5, :])
+    TR[1:2, :] = jnp.exp(RA[0, 3:4, :CH] - TR[4:5, :])
     column = jnp.transpose(TR[...])
     c_d3(0).wait_recv()
     QS[:CH, :] = (QG0[:CH, :] * column[:, 0:1] + DR2[:CH, :].astype(F32) * column[:, 1:2]).astype(BF16)
@@ -377,8 +399,8 @@
         y = x - 5 * nk
         c = jnp.where(first, x // 5, y // 4)
         v = jnp.where(first, lax.rem(x, 5), 6 + lax.rem(y + 8 * nk, 4))
-        lg = (v == 2) | (v == 7) | ((v == 1) & odd) | ((v == 8) & even)
         later = (c > 0) | (v >= 6)
+        lg = ((v == 2) & later) | (v == 7) | ((v == 1) & odd) | ((v == 8) & even)
         qg = later & ((v == 0) | (v == 3) | (v == 6) | (v == 9) | (((v == 1) | (v == 4)) & even))
 
         @pl.when(lg)
@@ -408,7 +430,7 @@
             YS[chunk(c), :] = GT[...].astype(BF16)
             send(c_yr, c)
 
-        @pl.when(v == 2)
+        @pl.when((v == 2) & later)
         def _():
             LS[chunk(c), :] = GT[...].astype(BF16)
             send(c_lz, c)
@@ -482,6 +504,26 @@
     loop(0, nk, drain_cores)
 
 
+def hand_over_kernel(*refs):
+    ins, outs, sems = refs[:3], refs[3:6], refs[6]
+    copies = [pltpu.make_async_copy(src, dst, sems.at[i]) for i, (src, dst) in enumerate(zip(ins, outs))]
+    for copy in copies:
+        copy.start()
+    for copy in copies:
+        copy.wait()
+
+
+def hand_over(*results):
+    return pl.pallas_call(
+        hand_over_kernel,
+        out_shape=tuple(jax.ShapeDtypeStruct(x.shape, x.dtype) for x in results),
+        in_specs=[pl.BlockSpec(memory_space=pltpu.VMEM)] * 3,
+        out_specs=(pl.BlockSpec(memory_space=pltpu.HBM),) * 3,
+        scratch_shapes=[pltpu.SemaphoreType.DMA((3,))],
+        compiler_params=pltpu.CompilerParams(vmem_limit_bytes=4 * 2**20),
+    )(*results)
+
+
 def local(queries, labels, logit_scale):
     rows, width = queries.shape
     nk, ns = rows // CH, rows // SUB
@@ -491,7 +533,7 @@
     loss, query_grad, label_grad = pl.pallas_call(
         kernel,
         out_shape=(
-            jax.ShapeDtypeStruct((1, rows), F32),
+            jax.ShapeDtypeStruct((rows,), F32),
             jax.ShapeDtypeStruct(block, BF16),
             jax.ShapeDtypeStruct(block, BF16),
         ),
@@ -527,7 +569,7 @@
             flops=6 * rows * 8 * rows * width, bytes_accessed=8 * rows * width, transcendentals=8 * rows * rows
         ),
     )(logit_scale, queries, labels)
-    return loss.reshape(rows), query_grad, label_grad
+    return hand_over(loss, query_grad, label_grad)
 
 
 def solution(mesh):

time: 82.4 us -> 78.7 us (0.955)
  local copies, waits for them, and re-layouts: 2.03 us -> 0 us
  Pallas kernels: 78.3 us -> 77.3 us
    unnamed x2 -> x0, local copies, waits for them, and re-layouts: 2.03 us -> none
    pallas_call x1 -> x2, Pallas kernels: 78.3 us -> 77.3 us  [the longest x1 75.9 us: local(): pl.pallas_call(kernel, out_shape=(jax.ShapeDtypeStruct((rows,), F32), jax...]
where the time goes in v3:
time: 78.7 us; the launch traced here: 78.6 us
  Pallas kernels  77.3 us (98%)
  between operations  1.28 us (2%)
    pallas_call x1, Pallas kernels, local(): pl.pallas_call(kernel, out_shape=(jax.ShapeDtypeStruct((rows,), F32), jax...  75.9 us

profile of v3, /device:TPU:1, one launch (start us, length us, event | category | flops | bytes accessed | tf_op | source)
XLA Modules:
  0.0 78.6 jit_solution(12400137608413466256)
XLA Ops:
  1.3 75.9 %shard_map.58 = (f32[768]{0:T(1024)S(1)}, bf16[768,768]{1,0:T(8,128)(2,1)S(1)}, bf16[768,768]{1,0:T(8,128)(2,1)S(1)}) custom-call(f32[1]{0:T(128)S(6)} %copy.6.scale_ref, bf16[768,768]{1,0:T(8,128)(2,1)} %q_ref.1, bf16[768,768]{1,0:T(8,128)(2,1)} %l_ref.1), custom_call_target="tpu_custom_call" | custom-call | flops 21743271936 | bytes 4718592 | tf_op jit(solution)/shard_map/pallas_call | solution.py:533
  77.1 1.4 %shard_map.59 = (f32[768]{0:T(1024)}, bf16[768,768]{1,0:T(8,128)(2,1)}, bf16[768,768]{1,0:T(8,128)(2,1)}) custom-call(f32[768]{0:T(1024)S(1)} %get-tuple-element.6.refs_0_, bf16[768,768]{1,0:T(8,128)(2,1)S(1)} %get-tuple-element.7.refs_1_, bf16[768,768]{1,0:T(8,128)(2,1)S(1)} %get-tuple-element.8.refs_2_), custom_call_target="tpu_custom_call" | custom-call | tf_op jit(solution)/shard_map/pallas_call | solution.py:517

commit v4 on v3

--- a/solution.py
+++ b/solution.py
@@ -12,6 +12,7 @@
 F32, BF16 = jnp.float32, jnp.bfloat16
 CH = 256
 SUB = 128
+PARTS = 4
 NT = (((1,), (1,)), ((), ()))
 NN = (((1,), (0,)), ((), ()))
 TN = (((0,), (0,)), ((), ()))
@@ -20,9 +21,9 @@
 
 def kernel(
     scale_ref, q_ref, l_ref, loss_ref, qg_ref, lg_ref,
-    B, E, MX, SM, AL, SA, SB, RA, RB, SII, TR, ACC, QG0, GT,
+    B, E, MX, SM, AL, SA, SB, SP, RA, RB, RP, SII, TR, ACC, QG0, GT,
     YS, LS, QS, DS3, DS5, DS1, YR, LR, QR, DR2, DR4, DR0,
-    s_in, s_q, r_q, s_l, r_l, s_y, r_y, s_1, r_1, s_3, r_3, s_5, r_5, s_sa, r_sa, s_sb, r_sb,
+    s_in, s_q, r_q, s_l, r_l, s_y, r_y, s_1, r_1, s_3, r_3, s_5, r_5, s_sa, r_sa, s_sb, r_sb, s_sp, r_sp,
     s_yr, r_yr, s_qz, r_qz, s_lz, r_lz, s_d3, r_d3, s_d5, r_d5, s_d1, r_d1,
 ):
     rows = q_ref.shape[0]
@@ -76,6 +77,9 @@
     def c_sa(j, dev):
         return rc(SA, RA.at[j], s_sa.at[j], r_sa.at[j], dev)
 
+    def c_sp(i, j, dev):
+        return rc(SP, RP.at[j], s_sp.at[i], r_sp.at[j], dev)
+
     def c_sb(i, j, dev):
         return rc(SB, RB.at[j], s_sb.at[i], r_sb.at[j], dev)
 
@@ -198,24 +202,71 @@
             square_piece(h, jnp.minimum(i, kk), jnp.where(i < kk, kk, i - kk))
 
     loop(0, 8 * nk, phase1)
+    def join(*parts):
+        top = functools.reduce(jnp.maximum, parts)
+        return top + jnp.log(sum(jnp.exp(part - top) for part in parts))
+
+    def of_terms(lo, hi):
+        m = functools.reduce(jnp.maximum, [MX[k, lo:hi, :] for k in range(nk)])
+        return m + jnp.log(sum(SM[k, lo:hi, :] * jnp.exp(MX[k, lo:hi, :] - m) for k in range(nk)))
+
+    def near():
+        return [c_sa(0, dev_d), c_sa(1, dev_q), c_sa(2, dev_qd)]
+
+    def far_own():
+        return [c_sp(0, 2, (at(-2), n)), c_sp(1, 3, (at(-2), nc))]
+
+    def far_passed():
+        return [
+            c_sb(1, 1, (at(3), n)), c_sb(2, 2, (at(3), nc)), c_sb(3, 1, (at(2), n)), c_sb(4, 2, (at(2), nc)),
+            c_sb(0, 0, dev_d),
+        ]
+
+    def far_got():
+        return [c_sp(0, 0, (at(-3), n)), c_sp(1, 1, (at(-3), nc))]
+
+    def each(copies, act):
+        for copy in copies:
+            act(copy)
+
+    @pl.when(even)
+    def _():
+        SP[...] = of_terms(0, 2)
+        each(far_own(), lambda copy: copy.start())
+
     edge = (nk - 1) * CH
 
-    def last_queries(h, upto):
-        for t in (1, 2, 3):
-            d = scores(t, h, 0, upto, edge, CH)
-            for k in range(upto // CH):
-                put(2 * t + h, k, slice(edge, rows), d[k * CH : (k + 1) * CH])
-
-    def last_labels(h, upto):
-        for t in (1, 2, 3):
-            put(2 * t + h, nk - 1, slice(0, upto), scores(t, h, edge, CH, 0, upto))
-
-    last_queries(0, edge)
+    def last_queries(t, h, upto):
+        d = scores(t, h, 0, upto, edge, CH)
+        for k in range(upto // CH):
+            put(2 * t + h, k, slice(edge, rows), d[k * CH : (k + 1) * CH])
+
+    def last_labels(t, h, upto):
+        put(2 * t + h, nk - 1, slice(0, upto), scores(t, h, edge, CH, 0, upto))
+
+    for t in (1, 2, 3):
+        last_queries(t, 0, edge)
     loop((nk - 1) * per, ns, lambda i: c_l(i).wait_recv())
-    last_labels(0, rows)
-    last_labels(1, edge)
-    arrived((nk - 1) * per, ns)
-    last_queries(1, rows)
+    for i in range(3):
+        t = jnp.where(even, 1 + i, 1 + (i + 1) % 3)
+        last_labels(t, 0, rows)
+        last_labels(t, 1, edge)
+        if i == 0:
+            arrived((nk - 1) * per, ns)
+        last_queries(t, 1, rows)
+        if i == 0:
+
+            @pl.when(even)
+            def _():
+                SB[...] = of_terms(2, 4)
+                each(far_passed(), lambda copy: copy.start())
+
+        if i == 1:
+
+            @pl.when(odd)
+            def _():
+                SP[...] = join(of_terms(4, 6), of_terms(6, 8))
+                each(far_got(), lambda copy: copy.start())
 
     def lg_piece(t0, count, c, more=False):
         def term(i):
@@ -265,35 +316,9 @@
 
         loop(0, count, term)
 
-    def join(*parts):
-        top = functools.reduce(jnp.maximum, parts)
-        return top + jnp.log(sum(jnp.exp(part - top) for part in parts))
-
-    m = functools.reduce(jnp.maximum, [MX[k] for k in range(nk)])
-    of_term = m + jnp.log(sum(SM[k] * jnp.exp(MX[k] - m) for k in range(nk)))
-    third = of_term[2:4]
-    SA[0:2, :] = jnp.where(odd, join(of_term[0:2], third), of_term[0:2])
+    of_term = of_terms(0, 8)
+    SA[0:2, :] = jnp.where(odd, join(of_term[0:2], of_term[2:4]), of_term[0:2])
     SA[2:4, :] = join(of_term[4:6], of_term[6:8])
-    SB[...] = third
-
-    def near():
-        return [c_sa(0, dev_d), c_sa(1, dev_q), c_sa(2, dev_qd)]
-
-    def far_even():
-        return [
-            c_sb(1, 1, (at(3), n)), c_sb(2, 2, (at(3), nc)), c_sb(3, 1, (at(2), n)), c_sb(4, 2, (at(2), nc)),
-            c_sa(5, (at(-2), n)), c_sa(6, (at(-2), nc)), c_sb(0, 0, dev_d),
-        ]
-
-    def far_odd():
-        return [c_sa(3, (at(-3), n)), c_sa(4, (at(-3), nc))]
-
-    def each(copies, act):
-        for copy in copies:
-            act(copy)
-
-    pl.when(even)(lambda: each(far_even(), lambda copy: copy.start()))
-    pl.when(odd)(lambda: each(far_odd(), lambda copy: copy.start()))
     each(near(), lambda copy: copy.start())
 
     got = SA[2:4, :]
@@ -302,7 +327,7 @@
         AL[k] = jnp.exp(MX[k] - own_view)
 
     def early(i):
-        of_got = lax.rem(i, 2) == 0
+        of_got = i != 1
 
         @pl.when(of_got | even)
         def _():
@@ -318,11 +343,11 @@
             DS5[:CH, :] = GT[...].astype(BF16)
             c_d5(0).start()
 
-        @pl.when((i == 2) | ((i == 3) & even))
-        def _():
-            QG0[chunk(i - 2), :] = GT[...]
-
-    loop(0, 4, early)
+        @pl.when(i == 2)
+        def _():
+            QG0[:CH, :] = GT[...]
+
+    loop(0, 3, early)
 
     def swap(x):
         return jnp.concatenate([x[1:2], x[0:1]], axis=0)
@@ -360,15 +385,14 @@
 
     @pl.when(even)
     def _():
-        for j in (3, 4, 5, 6):
-            c_sa(j, dev_d).wait_recv()
+        for j in range(4):
+            c_sp(j, j, dev_d).wait_recv()
         c_sb(0, 0, dev_d).wait_recv()
         lse0 = join(*near0, *far)
-        lse2 = join(SB[...], swap(RB[0]), RA[5, 0:2, :], swap(RA[6, 0:2, :]), RA[3, 2:4, :], swap(RA[4, 2:4, :]))
+        lse2 = join(SB[...], swap(RB[0]), RP[0], swap(RP[1]), RP[2], swap(RP[3]))
         settle(0, [lse0, lse2])
         loss_ref[...] = (lse0[0:1] - sum(SII[k : k + 1, :] for k in range(nk))).reshape(rows)
-        TR[2:3, :] = jnp.exp(SB[0:1, :CH] - lse2[0:1, :CH])
-        TR[3:4, :] = jnp.exp(RB[0, 1:2, :CH] - lse2[0:1, :CH])
+        TR[2:3, :] = jnp.exp(RB[0, 1:2, :CH] - lse2[0:1, :CH])
 
     @pl.when(odd)
     def _():
@@ -383,16 +407,23 @@
     TR[0:1, :] = jnp.exp(SA[2:3, :CH] - TR[4:5, :])
     TR[1:2, :] = jnp.exp(RA[0, 3:4, :CH] - TR[4:5, :])
     column = jnp.transpose(TR[...])
+
+    @pl.when(even)
+    def _():
+        qg_piece(1, 1, 0, 0)
+        c_d5(0).wait_recv()
+        YS[:CH, :] = (GT[...] + DR4[:CH, :].astype(F32) * column[:, 2:3]).astype(BF16)
+        send(c_yr, 0)
+
+    @pl.when(odd)
+    def _():
+        lg_piece(3, 1, 0)
+        YS[:CH, :] = GT[...].astype(BF16)
+        send(c_yr, 0)
+
     c_d3(0).wait_recv()
     QS[:CH, :] = (QG0[:CH, :] * column[:, 0:1] + DR2[:CH, :].astype(F32) * column[:, 1:2]).astype(BF16)
     send(c_qz, 0)
-
-    @pl.when(even)
-    def _():
-        c_d5(0).wait_recv()
-        g = QG0[CH : 2 * CH, :] * column[:, 2:3] + DR4[:CH, :].astype(F32) * column[:, 3:4]
-        YS[:CH, :] = g.astype(BF16)
-        send(c_yr, 0)
 
     def phase3(x):
         first = x < 5 * nk
@@ -400,7 +431,7 @@
         c = jnp.where(first, x // 5, y // 4)
         v = jnp.where(first, lax.rem(x, 5), 6 + lax.rem(y + 8 * nk, 4))
         later = (c > 0) | (v >= 6)
-        lg = ((v == 2) & later) | (v == 7) | ((v == 1) & odd) | ((v == 8) & even)
+        lg = ((v == 2) & later) | (v == 7) | ((v == 1) & odd & later) | ((v == 8) & even)
         qg = later & ((v == 0) | (v == 3) | (v == 6) | (v == 9) | (((v == 1) | (v == 4)) & even))
 
         @pl.when(lg)
@@ -425,7 +456,7 @@
             DS5[chunk(c), :] = GT[...].astype(BF16)
             c_d5(c).start()
 
-        @pl.when((v == 1) & odd)
+        @pl.when((v == 1) & odd & later)
         def _():
             YS[chunk(c), :] = GT[...].astype(BF16)
             send(c_yr, c)
@@ -465,9 +496,35 @@
             QG0[chunk(c), :] = GT[...]
 
     loop(0, 9 * nk, phase3)
-    loop(0, nk, lambda c: c_d1(c).wait_recv())
+
+    def drain(i):
+        for copy in (c_q, c_l, c_y, c_3):
+            copy(i).wait_send()
+
+        @pl.when(even)
+        def _():
+            c_5(i).wait_send()
+
+    loop(0, ns, drain)
+    c_1().wait_send()
+    each(near(), lambda copy: copy.wait_send())
+    pl.when(even)(lambda: each(far_own() + far_passed(), lambda copy: copy.wait_send()))
+    pl.when(odd)(lambda: each(far_got(), lambda copy: copy.wait_send()))
+
+    def drain_cores(c):
+        c_d1(c).wait_recv()
+        c_d3(c).wait_send()
+        c_d1(c).wait_send()
+
+        @pl.when(even)
+        def _():
+            c_d5(c).wait_send()
+
+    loop(0, nk, drain_cores)
 
     def finish(i):
+        for copy in (c_yr, c_qz, c_lz):
+            copy(i).wait_send()
         c_yr(i).wait_recv()
         passed = YR[sub(i), :].astype(F32)
         c_qz(i).wait_recv()
@@ -479,34 +536,15 @@
 
     loop(0, ns, finish)
 
-    def drain(i):
-        for copy in (c_q, c_l, c_y, c_3, c_yr, c_qz, c_lz):
-            copy(i).wait_send()
-
-        @pl.when(even)
-        def _():
-            c_5(i).wait_send()
-
-    loop(0, ns, drain)
-    c_1().wait_send()
-    each(near(), lambda copy: copy.wait_send())
-    pl.when(even)(lambda: each(far_even(), lambda copy: copy.wait_send()))
-    pl.when(odd)(lambda: each(far_odd(), lambda copy: copy.wait_send()))
-
-    def drain_cores(c):
-        c_d3(c).wait_send()
-        c_d1(c).wait_send()
-
-        @pl.when(even)
-        def _():
-            c_d5(c).wait_send()
-
-    loop(0, nk, drain_cores)
-
 
 def hand_over_kernel(*refs):
     ins, outs, sems = refs[:3], refs[3:6], refs[6]
-    copies = [pltpu.make_async_copy(src, dst, sems.at[i]) for i, (src, dst) in enumerate(zip(ins, outs))]
+    copies = [pltpu.make_async_copy(ins[0], outs[0], sems.at[0, 0])]
+    step = ins[1].shape[0] // PARTS
+    for j in (1, 2):
+        for i in range(PARTS):
+            part = pl.ds(i * step, step)
+            copies.append(pltpu.make_async_copy(ins[j].at[part], outs[j].at[part], sems.at[j, i]))
     for copy in copies:
         copy.start()
     for copy in copies:
@@ -519,7 +557,7 @@
         out_shape=tuple(jax.ShapeDtypeStruct(x.shape, x.dtype) for x in results),
         in_specs=[pl.BlockSpec(memory_space=pltpu.VMEM)] * 3,
         out_specs=(pl.BlockSpec(memory_space=pltpu.HBM),) * 3,
-        scratch_shapes=[pltpu.SemaphoreType.DMA((3,))],
+        scratch_shapes=[pltpu.SemaphoreType.DMA((3, PARTS))],
         compiler_params=pltpu.CompilerParams(vmem_limit_bytes=4 * 2**20),
     )(*results)
 
@@ -529,7 +567,7 @@
     nk, ns = rows // CH, rows // SUB
     block = (rows, width)
     dma = pltpu.SemaphoreType.DMA
-    counts = [ns, ns, ns, 1, ns, ns, 7, 5, ns, ns, ns, nk, nk, nk]
+    counts = [ns, ns, ns, 1, ns, ns, 3, 5, 4, ns, ns, ns, nk, nk, nk]
     loss, query_grad, label_grad = pl.pallas_call(
         kernel,
         out_shape=(
@@ -551,8 +589,10 @@
             pltpu.VMEM((nk, 8, rows), F32),
             pltpu.VMEM((4, rows), F32),
             pltpu.VMEM((2, rows), F32),
-            pltpu.VMEM((7, 4, rows), F32),
+            pltpu.VMEM((2, rows), F32),
+            pltpu.VMEM((3, 4, rows), F32),
             pltpu.VMEM((3, 2, rows), F32),
+            pltpu.VMEM((4, 2, rows), F32),
             pltpu.VMEM((8, rows), F32),
             pltpu.VMEM((8, CH), F32),
             pltpu.VMEM(block, F32),

time: 78.7 us -> 78 us (level)
  Pallas kernels: 77.3 us -> 76.4 us
    pallas_call x1, Pallas kernels: 75.9 us -> 74.9 us  [local(): pl.pallas_call(kernel, out_shape=(jax.ShapeDtypeStruct((rows,), F32), jax...]
where the time goes in v4:
time: 78 us; the launch traced here: 77.8 us
  Pallas kernels  76.4 us (98%)
  between operations  1.45 us (2%)
    pallas_call x1, Pallas kernels, local(): pl.pallas_call(kernel, out_shape=(jax.ShapeDtypeStruct((rows,), F32), jax...  74.9 us

profile of v4, /device:TPU:1, one launch (start us, length us, event | category | flops | bytes accessed | tf_op | source)
XLA Modules:
  0.0 77.8 jit_solution(4005707544437735345)
XLA Ops:
  1.3 74.9 %shard_map.58 = (f32[768]{0:T(1024)S(1)}, bf16[768,768]{1,0:T(8,128)(2,1)S(1)}, bf16[768,768]{1,0:T(8,128)(2,1)S(1)}) custom-call(f32[1]{0:T(128)S(6)} %copy.6.scale_ref, bf16[768,768]{1,0:T(8,128)(2,1)} %q_ref.1, bf16[768,768]{1,0:T(8,128)(2,1)} %l_ref.1), custom_call_target="tpu_custom_call" | custom-call | flops 21743271936 | bytes 4718592 | tf_op jit(solution)/shard_map/pallas_call | solution.py:571
  76.2 1.5 %shard_map.59 = (f32[768]{0:T(1024)}, bf16[768,768]{1,0:T(8,128)(2,1)}, bf16[768,768]{1,0:T(8,128)(2,1)}) custom-call(f32[768]{0:T(1024)S(1)} %get-tuple-element.6.refs_0_, bf16[768,768]{1,0:T(8,128)(2,1)S(1)} %get-tuple-element.7.refs_1_, bf16[768,768]{1,0:T(8,128)(2,1)S(1)} %get-tuple-element.8.refs_2_), custom_call_target="tpu_custom_call" | custom-call | tf_op jit(solution)/shard_map/pallas_call | solution.py:555

commit v5 on v4

--- a/solution.py
+++ b/solution.py
@@ -113,11 +113,11 @@
     in_q.start()
     in_l.start()
     barrier = pltpu.get_barrier_semaphore()
-    for dev in (back_y, out_y, dev_l, dev_q, dev_qd, dev_d):
+    for dev in (back_y, dev_l, dev_q, dev_qd, dev_d):
         pl.semaphore_signal(barrier, inc=1, device_id=dev, device_id_type=MESH)
     in_q.wait()
     in_l.wait()
-    pl.semaphore_wait(barrier, 6)
+    pl.semaphore_wait(barrier, 5)
 
     def send_first(i):
         c_y(i).start()

time: 78 us -> 78 us (level)
  no operation moved by 1% of the time
where the time goes in v5:
time: 78 us; the launch traced here: 77.8 us
  Pallas kernels  76.3 us (98%)
  between operations  1.45 us (2%)
    pallas_call x1, Pallas kernels, local(): pl.pallas_call(kernel, out_shape=(jax.ShapeDtypeStruct((rows,), F32), jax...  74.8 us

profile of v5, /device:TPU:1, one launch (start us, length us, event | category | flops | bytes accessed | tf_op | source)
XLA Modules:
  0.0 77.8 jit_solution(8639474392807891069)
XLA Ops:
  1.3 74.8 %shard_map.58 = (f32[768]{0:T(1024)S(1)}, bf16[768,768]{1,0:T(8,128)(2,1)S(1)}, bf16[768,768]{1,0:T(8,128)(2,1)S(1)}) custom-call(f32[1]{0:T(128)S(6)} %copy.6.scale_ref, bf16[768,768]{1,0:T(8,128)(2,1)} %q_ref.1, bf16[768,768]{1,0:T(8,128)(2,1)} %l_ref.1), custom_call_target="tpu_custom_call" | custom-call | flops 21743271936 | bytes 4718592 | tf_op jit(solution)/shard_map/pallas_call | solution.py:571
  76.1 1.5 %shard_map.59 = (f32[768]{0:T(1024)}, bf16[768,768]{1,0:T(8,128)(2,1)}, bf16[768,768]{1,0:T(8,128)(2,1)}) custom-call(f32[768]{0:T(1024)S(1)} %get-tuple-element.6.refs_0_, bf16[768,768]{1,0:T(8,128)(2,1)S(1)} %get-tuple-element.7.refs_1_, bf16[768,768]{1,0:T(8,128)(2,1)S(1)} %get-tuple-element.8.refs_2_), custom_call_target="tpu_custom_call" | custom-call | tf_op jit(solution)/shard_map/pallas_call | solution.py:555
